TPU v7x, 256 devices: a whole 4x4x8 slice. The times are simulated.
256 devices in a mesh: rep: 8 (over z), own: 32 (over x, y, core).
Axes of the slice: x: 4, y: 4, z: 8, core: 2. Of those that a mesh axis runs over, the one named last changes fastest.
Arguments:
- lambda_amp: float32 [8192, 3072], P('own', 'rep'), may hold values from -7 to 7
- lambda_tiles: int32 [8192, 24], P('own', 'rep'), may hold values 0 or 1
- integrals: float32 [3072, 3072], P(('rep', 'own')), may hold values from -100 to 100
- integral_tiles: int32 [24, 24], replicated, may hold values 0 or 1
Outputs:
- residual: float32 [8192, 3072], P('own', 'rep')
All inputs are finite; a program needn't handle non-finite values. No bound on the sum of `lambda_tiles` on one device may be relied on, other than what follows from the above.
Results may differ from a plain program's by a relative error of at most 0.0003.
Values may be sent and summed in bfloat16 or wider, within the bound.
A program may use at most 64 MiB of HBM per device.

v0:
```python
import jax
import jax.numpy as jnp
from jax import lax
from jax.sharding import PartitionSpec as P


def split_three(values):
    first = values.astype(jnp.bfloat16)
    first_wide = lax.optimization_barrier(first).astype(jnp.float32)
    rest = values - first_wide
    second = rest.astype(jnp.bfloat16)
    second_wide = lax.optimization_barrier(second).astype(jnp.float32)
    rest = rest - second_wide
    third = rest.astype(jnp.bfloat16)
    return (first, second, third)


def slice_product(left, right):
    pairs = ((0, 0), (0, 1), (1, 0), (0, 2), (1, 1), (2, 0))
    total = jnp.dot(left[0], right[0], preferred_element_type=jnp.float32)
    for first, second in pairs[1:]:
        total = total + jnp.dot(left[first], right[second], preferred_element_type=jnp.float32)
    return total


def per_device(lambda_amp, lambda_tiles, integrals, integral_tiles):
    tile_width = lambda_amp.shape[1] // lambda_tiles.shape[1]
    tile_count = integral_tiles.shape[0]
    keep = jnp.repeat(lambda_tiles.astype(jnp.float32), tile_width, axis=1)
    left = split_three(lambda_amp * keep)
    local_rows = integrals.shape[0]
    first_row = (lax.axis_index("rep") * lax.axis_size("own") + lax.axis_index("own")) * local_rows
    row_tile = (first_row + jnp.arange(local_rows, dtype=jnp.int32)) // tile_width
    onehot = (row_tile[:, None] == jnp.arange(tile_count, dtype=jnp.int32)[None, :]).astype(
        jnp.float32
    )
    row_flags = jnp.dot(
        onehot, integral_tiles.astype(jnp.float32), preferred_element_type=jnp.float32
    )
    masked = integrals * jnp.repeat(row_flags, tile_width, axis=1)
    right = split_three(masked)
    columns = tuple((part for part in left))
    partial_sum = slice_product(
        columns,
        (
            lax.all_gather(right[0], "own", axis=0, tiled=True),
            lax.all_gather(right[1], "own", axis=0, tiled=True),
            lax.all_gather(right[2], "own", axis=0, tiled=True),
        ),
    )
    return lax.psum_scatter(partial_sum, "rep", scatter_dimension=1, tiled=True)


def solution(mesh):
    placed = (P("own", "rep"), P("own", "rep"), P(("rep", "own"), None), P())
    return jax.shard_map(
        per_device, mesh=mesh, in_specs=placed, out_specs=P("own", "rep"), check_vma=False
    )
```

profile of v0, /device:TPU:1, one launch (start us, length us, event | category | flops | bytes accessed | tf_op | source)
XLA Modules:
  0.0 230.1 jit_solution(13912694934299906938)
XLA Ops:
  6.5 0.9 fusion.4
  7.4 0.1 broadcast_in_dim.9
  7.6 1.6 fusion.7
  9.3 1.5 fusion.2
  10.9 0.0 all-gather.11.cloned.1.call-start
  10.9 1.6 fusion.3
  12.6 0.7 convert_element_type.37
  13.3 1.2 copy.7
  14.5 0.1 fusion.1
  14.6 0.1 subtract_convert_fusion
  14.6 49.6 %all-gather.7.cloned.1.call-done = bf16[32,12,3072]{2,1,0:T(8,128)(2,1)} async-done(((bf16[1,12,3072]{2,1,0:T(8,128)(2,1)}), bf16[32,12,3072]{2,1,0:T(8,128)(2,1)}) %all-gather.7.cloned.1.call-update) | async-done | bytes 2359312 | tf_op jit(solution)/shard_map/all_gather | solution.py:46
  64.2 2.8 %reshape.28 = bf16[384,3072]{1,0:T(8,128)(2,1)S(1)} reshape(bf16[32,12,3072]{2,1,0:T(8,128)(2,1)} %all-gather.7.cloned.1.call-done) | data formatting | bytes 4718592
  67.1 49.2 %all-gather.9.cloned.1.call-done = bf16[32,12,3072]{2,1,0:T(8,128)(2,1)} async-done(((bf16[1,12,3072]{2,1,0:T(8,128)(2,1)}), bf16[32,12,3072]{2,1,0:T(8,128)(2,1)}) %all-gather.9.cloned.1.call-update) | async-done | bytes 2359312 | tf_op jit(solution)/shard_map/all_gather | solution.py:47
  116.3 4.3 %reshape.30 = bf16[384,3072]{1,0:T(8,128)(2,1)} reshape(bf16[32,12,3072]{2,1,0:T(8,128)(2,1)} %all-gather.9.cloned.1.call-done) | data formatting | bytes 4718592
  120.6 1.0 fusion.8
  121.6 0.7 copy-done
  122.3 1.0 convolution_add_fusion.4
  123.3 2.7 %convolution_add_fusion.3 = f32[256,3072]{1,0:T(8,128)} fusion(f32[256,3072]{1,0:T(8,128)S(1)} %convolution_add_fusion.4, bf16[256,384]{0,1:T(8,128)(2,1)S(1)} %fusion.1, bf16[384,3072]{1,0:T(8,128)(2,1)S(1)} %reshape.28), kind=kOutput, calls=%fused_computation.3 | convolution fusion | flops 604766208 | bytes 8847360 | tf_op jit(solution)/shard_map/dot_general | solution.py:22
  126.0 42.4 %all-gather.11.cloned.1.call-done = bf16[32,12,3072]{2,1,0:T(8,128)(2,1)} async-done(((bf16[1,12,3072]{2,1,0:T(8,128)(2,1)}), bf16[32,12,3072]{2,1,0:T(8,128)(2,1)}) %all-gather.11.cloned.1.call-update) | async-done | bytes 2359312 | tf_op jit(solution)/shard_map/all_gather | solution.py:48
  168.4 4.3 %reshape.32 = bf16[384,3072]{1,0:T(8,128)(2,1)} reshape(bf16[32,12,3072]{2,1,0:T(8,128)(2,1)} %all-gather.11.cloned.1.call-done) | data formatting | bytes 4718592
  172.8 3.8 %convolution_add_fusion.2 = f32[256,3072]{1,0:T(8,128)S(1)} fusion(f32[256,3072]{1,0:T(8,128)} %convolution_add_fusion.3, bf16[256,384]{0,1:T(8,128)(2,1)S(1)} %fusion, bf16[384,3072]{1,0:T(8,128)(2,1)} %reshape.32), kind=kOutput, calls=%fused_computation.2 | convolution fusion | flops 604766208 | bytes 8847360 | tf_op jit(solution)/shard_map/dot_general | solution.py:22
  176.6 1.0 convolution_add_fusion.1
  177.6 2.7 %convolution_add_fusion = f32[256,3072]{1,0:T(8,128)} fusion(f32[256,3072]{1,0:T(8,128)S(1)} %convolution_add_fusion.1, bf16[256,384]{0,1:T(8,128)(2,1)S(1)} %subtract_convert_fusion, bf16[384,3072]{1,0:T(8,128)(2,1)S(1)} %reshape.28), kind=kOutput, calls=%fused_computation | convolution fusion | flops 604766208 | bytes 8847360 | tf_op jit(solution)/shard_map/dot_general | solution.py:22
  180.3 43.3 %reduce-scatter.2.cloned.1.call-done = f32[256,384]{1,0:T(8,128)} async-done(((f32[256,3072]{1,0:T(8,128)}), f32[256,384]{1,0:T(8,128)}) %reduce-scatter.2.cloned.1.call-update) | async-done | bytes 393232 | tf_op jit(solution)/shard_map/reduce_scatter | solution.py:51
  (14 shorter events, 0.3 us)
Async XLA Ops:
  6.5 57.7 %all-gather.7.cloned.1.call-start = ((), (), s32[]{:S(2)}) async-start(), calls=%async_computation.2 | async-start | bytes 3244032 | tf_op jit(solution)/shard_map/all_gather | solution.py:46
  9.2 107.1 %all-gather.9.cloned.1.call-start = ((), (), s32[]{:S(2)}) async-start(), calls=%async_computation.3 | async-start | bytes 3244032 | tf_op jit(solution)/shard_map/all_gather | solution.py:47
  10.9 157.6 %all-gather.11.cloned.1.call-start = ((), (), s32[]{:S(2)}) async-start(), calls=%async_computation.4 | async-start | bytes 3244032 | tf_op jit(solution)/shard_map/all_gather | solution.py:48
  12.6 211.0 %reduce-scatter.2.cloned.1.call-start = ((), (), s32[]{:S(2)}) async-start(), calls=%async_computation.1 | async-start | bytes 3538944 | tf_op jit(solution)/shard_map/reduce_scatter | solution.py:51
  120.6 1.7 copy-start
  172.8 3.8 %copy-start.1 = (bf16[384,3072]{1,0:T(8,128)(2,1)S(1)}, bf16[384,3072]{1,0:T(8,128)(2,1)}, u32[]{:S(2)}) copy-start(bf16[384,3072]{1,0:T(8,128)(2,1)} %reshape.30) | copy-start | bytes 7077892
Sparse Core Ops, SparseCore 0:
  9.9 54.2 all-gather.6
  66.8 49.5 all-gather.8
  118.9 49.5 all-gather.10
  180.4 43.0 reduce-scatter.1
where the time goes:
time: 233 us; the launch traced here: 230 us
  waiting for transfers between devices  185 us (79%)
  local copies, waits for them, and re-layouts  13.4 us (6%)
  between operations  13.2 us (6%)
  matrix products  13.1 us (6%)
  other arithmetic  5.62 us (2%)
    all_gather x1, waiting for transfers between devices, per_device(): lax.all_gather(right[0], 'own', axis=0, tiled=True)  49.6 us
    all_gather x1, waiting for transfers between devices, per_device(): lax.all_gather(right[1], 'own', axis=0, tiled=True)  49.2 us
    reduce_scatter x1, waiting for transfers between devices, per_device(): return lax.psum_scatter(partial_sum, 'rep', scatter_dimension=1, tiled=True)  43.3 us
    all_gather x1, waiting for transfers between devices, per_device(): lax.all_gather(right[2], 'own', axis=0, tiled=True)  42.4 us
    unnamed x10, local copies, waits for them, and re-layouts  13.3 us
    dot_general x5, matrix products, slice_product(): jnp.dot(left[first], right[second], preferred_element_type=jnp.float32)  11.2 us
  transfers between devices with their start and end apart: 4, of which 4 were waited for; matrix products, arithmetic and copies ran while one was open for 7% of the time, Pallas kernels for 0%

commit v1 on v0

v1 whole, which is shorter than its diff:
```python
import jax
import jax.numpy as jnp
from jax import lax
from jax.experimental import pallas as pl
from jax.experimental.pallas import tpu as pltpu
from jax.sharding import PartitionSpec as P

MESH = pl.DeviceIdType.MESH
F32, BF16, I32, I16 = jnp.float32, jnp.bfloat16, jnp.int32, jnp.int16
TILE = 128
W = 384
ROWS = 256
SUB = 128
Q = 32767.0


def split3(v):
    first = v.astype(BF16)
    rest = v - first.astype(F32)
    second = rest.astype(BF16)
    rest = rest - second.astype(F32)
    return first, second, rest.astype(BF16)


def encode(v):
    top = jnp.maximum(jnp.max(jnp.abs(v), axis=0, keepdims=True), 1e-30)
    code = jnp.round(v * (Q / top)).astype(I32).astype(I16)
    return code, top * (1.0 / Q)


def decode(code, scale):
    return code.astype(I32).astype(F32) * scale


def kernel(
    lam_hbm, keep_hbm, ints_hbm, flags, out,
    lam, keep, ints, lamx, ge, he, gp, hp, la, lb, ra, part, own_part,
    sq, ss, rq, rs, fq, fs,
    in_sem, s1, r1, s2, r2, sf, rf, sl, rl, szq, szs, rzq, rzs, rfq, rfs,
):
    z = lax.axis_index("rep")
    own = lax.axis_index("own")
    core = lax.rem(own, 2)
    x = own // 8
    y = lax.rem(own // 2, 4)
    a = x + core * (y - x)
    b = y + core * (x - y)
    step = 1 - 2 * core

    def at(dz, da, db, c):
        aa, bb = lax.rem(a + da, 4), lax.rem(b + db, 4)
        xx, yy = aa + core * (bb - aa), bb + core * (aa - bb)
        return (lax.rem(z + dz + 8, 8), (xx * 4 + yy) * 2 + c)

    def chunk(distance, c):
        return lax.rem(z + distance * (1 - 2 * c) + 8, 8)

    def remote(src, dst, send, recv, device):
        return pltpu.make_async_remote_copy(
            src_ref=src, dst_ref=dst, send_sem=send, recv_sem=recv, device_id=device, device_id_type=MESH
        )

    loads = [
        pltpu.make_async_copy(ints_hbm, ints, in_sem.at[0]),
        pltpu.make_async_copy(lam_hbm, lam, in_sem.at[1]),
        pltpu.make_async_copy(keep_hbm, keep, in_sem.at[2]),
    ]
    for load in loads:
        load.start()

    barrier = pltpu.get_barrier_semaphore()
    peers = [at(0, 0, 0, 1 - core)]
    peers += [at(0, t, 0, core) for t in (1, 2, 3)] + [at(0, 0, t, core) for t in (1, 2, 3)]
    peers += [at(step, 0, 0, core), at(-step, 0, 0, core), at(step, 0, 0, 1 - core)]
    for peer in peers:
        pl.semaphore_signal(barrier, inc=1, device_id=peer, device_id_type=MESH)

    loads[0].wait()
    first_row = own * 12
    t0 = first_row // TILE
    t1 = (first_row + 11) // TILE
    bound = (t0 + 1) * TILE - first_row
    above = lax.broadcasted_iota(I32, (12, TILE), 0) < bound
    for j in range(24):
        f0 = flags[3 * z + t0, j].astype(F32)
        f1 = flags[3 * z + t1, j].astype(F32)
        ints[:, j * TILE : (j + 1) * TILE] = ints[:, j * TILE : (j + 1) * TILE] * jnp.where(above, f0, f1)

    def columns(ch):
        return pl.ds(pl.multiple_of(ch * W, TILE), W)

    for e, distance in ((0, 4), (1, 0)):
        cols = columns(chunk(distance, core))
        ge[e, a, b, 0] = ints[0:8, cols]
        ge[e, a, b, 1, 0:4] = ints[8:12, cols]
        ge[e, a, b, 1, 4:8] = ints[8:12, cols]
    for p in range(3):
        gp[p, a, b, 0] = ints[0:8, columns(chunk(3 - p, 0))]
        gp[p, a, b, 2] = ints[0:8, columns(chunk(3 - p, 1))]
        gp[p, a, b, 1, 0:4] = ints[8:12, columns(chunk(3 - p, core))]
        gp[p, a, b, 1, 4:8] = ints[8:12, columns(chunk(3 - p, 1 - core))]

    loads[1].wait()
    loads[2].wait()
    for u in range(3):
        cols = slice(u * TILE, (u + 1) * TILE)
        lam[:, cols] = lam[:, cols] * keep[:, u : u + 1].astype(F32)

    def gathered(g):
        return ge.at[(0, None, None, None, 1)[g]] if g in (0, 4) else gp.at[g - 1]

    def handed(g):
        return he.at[(0, None, None, None, 1)[g]] if g in (0, 4) else hp.at[g - 1]

    def phase1(g, t):
        mine = gathered(g).at[a, b]
        return remote(mine, mine, s1.at[g, t - 1], r1.at[g, t - 1], at(0, 0, t, core))

    def phase2(g, t):
        mine = gathered(g).at[a]
        return remote(mine, mine, s2.at[g, t - 1], r2.at[g, t - 1], at(0, t, 0, core))

    def handing(g, t):
        aa = lax.rem(a + 4 - t, 4)
        if g in (0, 4):
            src = gathered(g).at[aa]
        else:
            src = gathered(g).at[aa, :, pl.ds(1 - core, 2)]
        return remote(src, handed(g).at[aa], sf.at[g, t], rf.at[g, t], at(0, 0, 0, 1 - core))

    def start1(g):
        for t in (1, 3, 2):
            phase1(g, t).start()

    def start2(g):
        for t in (1, 3, 2):
            phase1(g, t).wait_recv()
        for t in (1, 3, 2):
            phase2(g, t).start()
        handing(g, 0).start()

    def hand(g):
        for t in (1, 3, 2):
            phase2(g, t).wait_recv()
            handing(g, t).start()

    def arrived(g):
        for t in range(4):
            handing(g, t).wait_recv()

    lam_copy = remote(lam, lamx, sl, rl, at(0, 0, 0, 1 - core))

    pl.semaphore_wait(barrier, len(peers))
    start1(0)
    lam_copy.start()
    start1(1)

    n = lax.broadcasted_iota(I32, (1, W), 1)
    m = n & 127
    ia, ib, r = m >> 5, (m >> 3) & 3, m & 7
    up, down = ia * 4 + ib, ib * 4 + ia
    mine = 24 * (up + core * (down - up)) + 12 * core
    theirs = 24 * (down + core * (up - down)) + 12 * (1 - core)
    tail = jnp.where(r < 4, mine + 8 + r, theirs + 4 + r)
    place = jnp.where(n < 128, mine + r, jnp.where(n < 256, theirs + r, tail))
    order = (lax.broadcasted_iota(I32, (W, W), 0) == place).astype(BF16)

    def prepare(values, h):
        rows = slice(h * ROWS, (h + 1) * ROWS)
        l1, l2, l3 = (jnp.dot(s, order, preferred_element_type=F32).astype(BF16) for s in split3(values))
        for i, s in enumerate((l1, l1, l1, l3)):
            la[rows, i * W : (i + 1) * W] = s
        for i in range(2):
            lb[rows, i * W : (i + 1) * W] = l2

    prepare(lam[...], 0)
    start2(0)
    start1(2)
    start1(3)
    start1(4)
    start2(1)
    lam_copy.wait_recv()
    prepare(lamx[...], 1)

    def right(g):
        if g in (0, 4):
            mine, theirs = gathered(g), handed(g)
            places = (0, 1), (0, 1)
        else:
            mine, theirs = gathered(g), handed(g)
            places = (2 * core, 1), (core, 1 - core)
        low = lax.broadcasted_iota(I32, (16, 8, W), 1) < 4

        def piece(ref, place):
            return ref[:, :, place].reshape(16, 8, W)

        parts = (
            piece(mine, places[0][0]),
            piece(theirs, places[1][0]),
            jnp.where(low, piece(mine, places[0][1]), piece(theirs, places[1][1])),
        )
        for i, v in enumerate(parts):
            r1_, r2_, r3_ = split3(v.reshape(128, W))
            for k, s in enumerate((r1_, r2_, r3_, r1_)):
                ra[k * W + i * 128 : k * W + (i + 1) * 128] = s

    def product(h):
        rows = slice(h * ROWS, (h + 1) * ROWS)
        total = jnp.dot(la[rows], ra[...], preferred_element_type=F32)
        return total + jnp.dot(lb[rows], ra[0 : 2 * W], preferred_element_type=F32)

    def sends(j, h, u):
        if j < 3:
            target = at(step, 0, 0, core)
            to = (rq.at[j, h, u], rs.at[j, h, u], rzq.at[j, h, u], rzs.at[j, h, u])
        else:
            target = at(step, 0, 0, core if h == 0 else 1 - core)
            to = (fq.at[core, u], fs.at[core, u], rfq.at[core, u], rfs.at[core, u])
        return (
            remote(sq.at[j, h, u], to[0], szq.at[j, h, u], to[2], target),
            remote(ss.at[j, h, u], to[1], szs.at[j, h, u], to[3], target),
        )

    def receive(j, h, u):
        for copy in sends(j, h, u):
            copy.wait_recv()
        return decode(rq[j, h, u], rs[j, h, u])

    def pass_on(j, h, u, came):
        v = part[(h * 2 + u) * SUB : (h * 2 + u + 1) * SUB]
        if came:
            v = v + receive(j - 1, h, u)
        code, scale = encode(v)
        sq[j, h, u] = code
        ss[j, h, u] = scale
        for copy in sends(j, h, u):
            copy.start()

    hand(0)
    start2(2)
    arrived(0)
    right(0)
    part[0:ROWS] = product(0)
    for u in range(2):
        pass_on(0, 0, u, False)

    for j in (1, 2, 3):
        hand(j)
        if j < 3:
            start2(j + 2)
        arrived(j)
        right(j)
        for h in (1, 0):
            part[h * ROWS : (h + 1) * ROWS] = product(h)
        for h in (1, 0):
            for u in range(2):
                pass_on(j, h, u, j > 1 or h == 0)

    hand(4)
    arrived(4)
    right(4)
    own_part[...] = product(0)
    for u in range(2):
        rows = slice(u * SUB, (u + 1) * SUB)
        v = own_part[rows]
        for c in range(2):
            for ref, sem in ((fq, rfq), (fs, rfs)):
                remote(ref.at[c, u], ref.at[c, u], szq.at[3, 0, u], sem.at[c, u], at(step, 0, 0, core)).wait_recv()
            v = v + decode(fq[c, u], fs[c, u])
        out[rows] = v

    lam_copy.wait_send()
    for g in range(5):
        for t in (1, 2, 3):
            phase1(g, t).wait_send()
            phase2(g, t).wait_send()
        for t in range(4):
            handing(g, t).wait_send()
    for j in range(4):
        for h in range(2):
            for u in range(2):
                if j > 0 or h == 0:
                    for copy in sends(j, h, u):
                        copy.wait_send()


def per_device(lambda_amp, lambda_tiles, integrals, integral_tiles):
    dma = pltpu.SemaphoreType.DMA
    hbm = pl.BlockSpec(memory_space=pl.ANY)
    return pl.pallas_call(
        kernel,
        out_shape=jax.ShapeDtypeStruct((ROWS, W), F32),
        in_specs=[hbm, hbm, hbm, pl.BlockSpec(memory_space=pltpu.SMEM)],
        out_specs=pl.BlockSpec(memory_space=pltpu.VMEM),
        scratch_shapes=[
            pltpu.VMEM((ROWS, W), F32),
            pltpu.VMEM((ROWS, 3), I32),
            pltpu.VMEM((12, 8 * W), F32),
            pltpu.VMEM((ROWS, W), F32),
            pltpu.VMEM((2, 4, 4, 2, 8, W), F32),
            pltpu.VMEM((2, 4, 4, 2, 8, W), F32),
            pltpu.VMEM((3, 4, 4, 3, 8, W), F32),
            pltpu.VMEM((3, 4, 4, 2, 8, W), F32),
            pltpu.VMEM((2 * ROWS, 4 * W), BF16),
            pltpu.VMEM((2 * ROWS, 2 * W), BF16),
            pltpu.VMEM((4 * W, W), BF16),
            pltpu.VMEM((2 * ROWS, W), F32),
            pltpu.VMEM((ROWS, W), F32),
            pltpu.VMEM((4, 2, 2, SUB, W), I16),
            pltpu.VMEM((4, 2, 2, 1, W), F32),
            pltpu.VMEM((3, 2, 2, SUB, W), I16),
            pltpu.VMEM((3, 2, 2, 1, W), F32),
            pltpu.VMEM((2, 2, SUB, W), I16),
            pltpu.VMEM((2, 2, 1, W), F32),
            dma((3,)),
            dma((5, 3)),
            dma((5, 3)),
            dma((5, 3)),
            dma((5, 3)),
            dma((5, 4)),
            dma((5, 4)),
            dma,
            dma,
            dma((4, 2, 2)),
            dma((4, 2, 2)),
            dma((3, 2, 2)),
            dma((3, 2, 2)),
            dma((2, 2)),
            dma((2, 2)),
        ],
        compiler_params=pltpu.CompilerParams(
            collective_id=0, has_side_effects=True, vmem_limit_bytes=48 << 20
        ),
        cost_estimate=pl.CostEstimate(flops=3_700_000_000, bytes_accessed=1_500_000, transcendentals=0),
    )(lambda_amp, lambda_tiles, integrals, integral_tiles)


def solution(mesh):
    placed = (P("own", "rep"), P("own", "rep"), P(("rep", "own"), None), P())
    return jax.shard_map(
        per_device, mesh=mesh, in_specs=placed, out_specs=P("own", "rep"), check_vma=False
    )
```

time: 233 us -> 47 us (0.20); the launches traced: 230 us -> 46.9 us
  waiting for transfers between devices: 185 us -> 0 us
  Pallas kernels: 0 us -> 43.3 us
  between operations: 13.2 us -> 0.03 us
  matrix products: 13.1 us -> 0 us
  local copies, waits for them, and re-layouts: 13.4 us -> 3.5 us
  other arithmetic: 5.62 us -> 0 us
    all_gather x3 -> x0, waiting for transfers between devices: 141 us -> none  [the longest x1 49.6 us: per_device(): lax.all_gather(right[0], 'own', axis=0, tiled=True)]
    pallas_call x0 -> x1, Pallas kernels: none -> 43.3 us  [per_device(): pl.pallas_call(kernel, out_shape=jax.ShapeDtypeStruct((ROWS, W), F32), in...]
    reduce_scatter x1 -> x0, waiting for transfers between devices: 43.3 us -> none  [per_device(): return lax.psum_scatter(partial_sum, 'rep', scatter_dimension=1, tiled=True)]
    dot_general x7 -> x0, matrix products: 13.1 us -> none  [the longest x5 11.2 us: slice_product(): jnp.dot(left[first], right[second], preferred_element_type=jnp.float32)]
    unnamed x10 -> x8, local copies, waits for them, and re-layouts: 13.3 us -> 3.5 us
    convert_element_type x6 -> x0, other arithmetic: 4 us -> none  [the longest x2 1.63 us: split_three(): first = values.astype(jnp.bfloat16)]
  transfers between devices with their start and end apart: 4 -> 0, of which waited for: 4 -> 0; matrix products, arithmetic and copies ran while one was open for 7% -> 0% of each run, Pallas kernels for 0% -> 0%
where the time goes in v1:
time: 47 us; the launch traced here: 46.9 us
  Pallas kernels  43.3 us (92%)
  local copies, waits for them, and re-layouts  3.5 us (7%)
    pallas_call x1, Pallas kernels, per_device(): pl.pallas_call(kernel, out_shape=jax.ShapeDtypeStruct((ROWS, W), F32), in...  43.3 us
    unnamed x8, local copies, waits for them, and re-layouts  3.5 us

profile of v1, /device:TPU:1, one launch (start us, length us, event | category | flops | bytes accessed | tf_op | source)
XLA Modules:
  0.0 46.9 jit_solution(15273011925548597173)
XLA Ops:
  0.0 0.0 copy-start.2
  0.0 0.8 %copy.5.keep_hbm = s32[256,3]{1,0:T(8,128)S(1)} copy(s32[256,3]{0,1:T(4,128)} %param.5) | data formatting | bytes 6144 | tf_op args[1]
  0.8 0.0 copy-done.2
  0.8 0.0 copy-start
  0.9 1.0 %copy-done = f32[256,384]{1,0:T(8,128)S(1)} copy-done((f32[256,384]{1,0:T(8,128)S(1)}, f32[256,384]{1,0:T(8,128)}, u32[]{:S(2)}) %copy-start) | copy-done | bytes 393240
  1.8 0.0 copy-start.1
  1.8 0.9 %copy-done.1 = f32[12,3072]{1,0:T(8,128)S(1)} copy-done((f32[12,3072]{1,0:T(8,128)S(1)}, f32[12,3072]{1,0:T(8,128)}, u32[]{:S(2)}) %copy-start.1) | copy-done | bytes 147480
  2.8 43.3 %shard_map.46 = f32[256,384]{1,0:T(8,128)S(1)} custom-call(f32[256,384]{1,0:T(8,128)S(1)} %copy-done, s32[256,3]{1,0:T(8,128)S(1)} %copy.5.keep_hbm, f32[12,3072]{1,0:T(8,128)S(1)} %copy-done.1, s32[24,24]{1,0:T(8,128)S(1)} %copy-done.2), custom_call_target="tpu_custom_call" | custom-call | flops 3700000000 | bytes 1500000 | tf_op jit(solution)/shard_map/pallas_call | solution.py:290
  46.1 0.7 %copy.7 = f32[256,384]{1,0:T(8,128)} copy(f32[256,384]{1,0:T(8,128)S(1)} %shard_map.46) | data formatting | bytes 786432
Async XLA Ops:
  0.0 0.8 %copy-start.2 = (s32[24,24]{1,0:T(8,128)S(1)}, s32[24,24]{1,0:T(8,128)}, u32[]{:S(2)}) copy-start(s32[24,24]{1,0:T(8,128)} %flags.1) | copy-start | bytes 6916
  0.8 1.0 %copy-start = (f32[256,384]{1,0:T(8,128)S(1)}, f32[256,384]{1,0:T(8,128)}, u32[]{:S(2)}) copy-start(f32[256,384]{1,0:T(8,128)} %lam_hbm.1) | copy-start | bytes 1179652
  1.8 0.9 %copy-start.1 = (f32[12,3072]{1,0:T(8,128)S(1)}, f32[12,3072]{1,0:T(8,128)}, u32[]{:S(2)}) copy-start(f32[12,3072]{1,0:T(8,128)} %ints_hbm.1) | copy-start | bytes 442372

commit v2 on v1

v2 whole, which is shorter than its diff:
```python
import jax
import jax.numpy as jnp
from jax import lax
from jax.experimental import pallas as pl
from jax.experimental.pallas import tpu as pltpu
from jax.sharding import PartitionSpec as P

MESH = pl.DeviceIdType.MESH
F32, BF16, I32, I16 = jnp.float32, jnp.bfloat16, jnp.int32, jnp.int16
TILE = 128
W = 384
ROWS = 256
SUB = 128
Q = 32767.0


def split3(v):
    first = v.astype(BF16)
    rest = v - first.astype(F32)
    second = rest.astype(BF16)
    rest = rest - second.astype(F32)
    return first, second, rest.astype(BF16)


def encode(v):
    top = jnp.maximum(jnp.max(jnp.abs(v), axis=0, keepdims=True), 1e-30)
    code = jnp.round(v * (Q / top)).astype(I32).astype(I16)
    return code, top * (1.0 / Q)


def decode(code, scale):
    return code.astype(I32).astype(F32) * scale


def kernel(
    lam_hbm, keep_hbm, ints_hbm, flags_hbm, out_hbm,
    lam, keep, ints, flags, lamx, came, relay, gath, la, lb, ra, part, result, total,
    sq, ss, rq, rs, fq, fs,
    in_sem, out_sem, s1, r1, s2, r2, sl, rl, so, ro, szq, szs, rzq, rzs, rfq, rfs,
):
    z = lax.axis_index("rep")
    own = lax.axis_index("own")
    core = lax.rem(own, 2)
    x = own // 8
    y = lax.rem(own // 2, 4)
    a = x + core * (y - x)
    b = y + core * (x - y)
    step = 1 - 2 * core

    def at(dz, da, db, c):
        aa, bb = lax.rem(a + da, 4), lax.rem(b + db, 4)
        xx, yy = aa + core * (bb - aa), bb + core * (aa - bb)
        return (lax.rem(z + dz + 8, 8), (xx * 4 + yy) * 2 + c)

    def chunk(distance, c):
        return lax.rem(z + distance * (1 - 2 * c) + 8, 8)

    def remote(src, dst, send, recv, device):
        return pltpu.make_async_remote_copy(
            src_ref=src, dst_ref=dst, send_sem=send, recv_sem=recv, device_id=device, device_id_type=MESH
        )

    barrier = pltpu.get_barrier_semaphore()
    peers = [at(0, t, 0, 1 - core) for t in range(4)] + [at(0, 0, t, 1 - core) for t in (1, 2, 3)]
    peers += [at(0, t, 0, core) for t in (1, 2, 3)] + [at(0, 0, t, core) for t in (1, 2, 3)]
    peers += [at(d, 0, 0, c) for d in (1, -1) for c in (core, 1 - core)]
    for peer in peers:
        pl.semaphore_signal(barrier, inc=1, device_id=peer, device_id_type=MESH)

    loads = [
        pltpu.make_async_copy(ints_hbm, ints, in_sem.at[0]),
        pltpu.make_async_copy(flags_hbm, flags, in_sem.at[1]),
        pltpu.make_async_copy(lam_hbm, lam, in_sem.at[2]),
        pltpu.make_async_copy(keep_hbm, keep, in_sem.at[3]),
    ]
    for load in loads:
        load.start()
    loads[0].wait()
    loads[1].wait()

    first_row = own * 12
    t0 = first_row // TILE
    t1 = (first_row + 11) // TILE
    bound = (t0 + 1) * TILE - first_row
    above = lax.broadcasted_iota(I32, (12, TILE), 0) < bound
    odd = lax.rem(b, 2)

    def masked(ch, u):
        cols = pl.ds(pl.multiple_of(ch * W + u * TILE, TILE), TILE)
        f0 = flags[3 * z + t0, 3 * ch + u].astype(F32)
        f1 = flags[3 * z + t1, 3 * ch + u].astype(F32)
        return ints[:, cols] * jnp.where(above, f0, f1)

    def pack(g):
        for u in range(3):
            to = slice(u * TILE, (u + 1) * TILE)
            if g in (0, 4):
                v = masked(chunk(4 - g, 0), u)
                came[g, b, 1, :, to] = v[0:8]
                came[g, b, 2, 0:4, to] = v[8:12]
                came[g, b, 2, 4:8, to] = v[8:12]
            else:
                v = masked(chunk(4 - g, odd), u)
                came[g, b, odd, :, to] = v[0:8]
                came[g, b, 2, 0:4, to] = v[8:12]
                v = masked(chunk(4 - g, 1 - odd), u)
                came[g, b, 1 - odd, :, to] = v[0:8]
                came[g, b, 2, 4:8, to] = v[8:12]

    for g in range(5):
        pack(g)

    def phase1(g, t, slot):
        rows = came.at[g, slot, pl.ds(1, 2)] if g in (0, 4) else came.at[g, slot]
        return remote(rows, rows, s1.at[g, t - 1], r1.at[g, slot], at(0, 0, t, core))

    def start1(g):
        for t in (1, 3, 2):
            phase1(g, t, b).start()

    def phase2(g, o, t):
        src = gath.at[g, core, a] if o == 0 else relay.at[g]
        return remote(src, gath.at[g, core, a], s2.at[g, o, t], r2.at[g, core, a], at(0, t, 0, core + o - 2 * core * o))

    def phase2_came(g, o, t):
        c, slot = (core, lax.rem(a + t, 4)) if o == 0 else (1 - core, lax.rem(b + t, 4))
        device = at(0, t, 0, c) if o == 0 else at(0, 0, t, c)
        return remote(gath.at[g, c, slot], gath.at[g, c, slot], s2.at[g, o, t], r2.at[g, c, slot], device)

    same, other = ((0, 1), (0, 3), (0, 2)), ((1, 1), (1, 3), (1, 2), (1, 0))
    low = lax.broadcasted_iota(I32, (8, W), 0) < 4
    mine_first = (lax.broadcasted_iota(I32, (8, W), 0) < 4) == (core == 0)

    def split_by_core(g, ours, theirs):
        pl.when(core == g // 4)(ours)
        pl.when(core != g // 4)(theirs)

    def start2(g):
        for t in (1, 3, 2):
            phase1(g, t, lax.rem(b + t, 4)).wait_recv()
        for i in range(4):
            gath[g, core, a, i] = came[g, i, 1 if g in (0, 4) else core]
            relay[g, i] = came[g, i, 1 if g in (0, 4) else 1 - core]
        for i in range(2):
            even, uneven = came[g, 2 * i, 2], came[g, 2 * i + 1, 2]
            if g in (0, 4):
                tail = jnp.where(low, even, uneven) if g == 0 else jnp.where(low, uneven, even)
                gath[g, core, a, 4 + i] = tail
                relay[g, 4 + i] = tail
            else:
                gath[g, core, a, 4 + i] = jnp.where(mine_first, even, uneven)
                relay[g, 4 + i] = jnp.where(mine_first, uneven, even)
        if g in (0, 4):
            split_by_core(
                g,
                lambda: [phase2(g, o, t).start() for o, t in same] and None,
                lambda: [phase2(g, o, t).start() for o, t in other] and None,
            )
        else:
            for o, t in same + other:
                phase2(g, o, t).start()

    def arrived(g):
        for o, t in same + other:
            phase2_came(g, o, t).wait_recv()

    lam_copy = remote(lam, lamx, sl, rl, at(0, 0, 0, 1 - core))

    pl.semaphore_wait(barrier, len(peers))
    start1(0)
    start1(1)

    loads[2].wait()
    loads[3].wait()
    kept = jnp.concatenate([keep[...].astype(F32), jnp.zeros((5, ROWS), F32)], axis=0).T
    for u in range(3):
        cols = slice(u * TILE, (u + 1) * TILE)
        lam[:, cols] = lam[:, cols] * kept[:, u : u + 1]
    lam_copy.start()
    start1(2)
    start1(3)
    start1(4)

    n = lax.broadcasted_iota(I32, (1, W), 1)
    origin = (n >= 192).astype(I32)
    n = n - 192 * origin
    ia = (n * 1366) >> 16
    n = n - 48 * ia
    tile, r = n >> 3, n & 7
    half = r >> 2
    ib = jnp.where(tile < 4, tile, 2 * (tile - 4) + half + core - 2 * core * half)
    chip = jnp.where(origin == 0, ia * 4 + ib, ib * 4 + ia)
    place = 24 * chip + 12 * origin + jnp.where(tile < 4, r, 8 + (r & 3))
    order = (lax.broadcasted_iota(I32, (W, W), 0) == place).astype(BF16)

    def prepare(values, h):
        rows = slice(h * ROWS, (h + 1) * ROWS)
        l1, l2, l3 = (jnp.dot(s, order, preferred_element_type=F32).astype(BF16) for s in split3(values))
        for i, s in enumerate((l1, l1, l1, l3)):
            la[rows, i * W : (i + 1) * W] = s
        for i in range(2):
            lb[rows, i * W : (i + 1) * W] = l2

    prepare(lam[...], 0)
    for g in range(4):
        start2(g)
    lam_copy.wait_recv()
    prepare(lamx[...], 1)

    def right(g):
        for i in range(8):
            r1_, r2_, r3_ = split3(gath[g, i // 4, i % 4].reshape(48, W))
            for k, s in enumerate((r1_, r2_, r3_, r1_)):
                ra[k * W + i * 48 : k * W + (i + 1) * 48] = s

    def product(h):
        rows = slice(h * ROWS, (h + 1) * ROWS)
        most = jnp.dot(la[rows], ra[...], preferred_element_type=F32)
        return most + jnp.dot(lb[rows], ra[0 : 2 * W], preferred_element_type=F32)

    def sends(j, h, u):
        if j < 3:
            target = at(step, 0, 0, core) if j else at(1 - 2 * h, 0, 0, h)
            hh = h if j else 0
            to = (rq.at[j, hh, u], rs.at[j, hh, u], rzq.at[j, hh, u], rzs.at[j, hh, u])
        else:
            target = at(step, 0, 0, core if h == 0 else 1 - core)
            to = (fq.at[core, u], fs.at[core, u], rfq.at[core, u], rfs.at[core, u])
        return (
            remote(sq.at[j, h, u], to[0], szq.at[j, h, u], to[2], target),
            remote(ss.at[j, h, u], to[1], szs.at[j, h, u], to[3], target),
        )

    def came_in(q_ref, s_ref, q_sem, s_sem):
        for ref, sem in ((q_ref, q_sem), (s_ref, s_sem)):
            remote(ref, ref, szq.at[3, 0, 0], sem, at(step, 0, 0, core)).wait_recv()
        return decode(q_ref[...], s_ref[...])

    def pass_on(j, h, u, add):
        v = part[(h * 2 + u) * SUB : (h * 2 + u + 1) * SUB]
        if add:
            at_ = (j - 1, h, u)
            v = v + came_in(rq.at[at_], rs.at[at_], rzq.at[at_], rzs.at[at_])
        code, scale = encode(v)
        sq[j, h, u] = code
        ss[j, h, u] = scale
        for copy in sends(j, h, u):
            copy.start()

    own_copy = remote(part.at[pl.ds(ROWS, ROWS)], result, so, ro, at(0, 0, 0, 1 - core))

    @pl.when(core == 0)
    def _():
        arrived(0)
        right(0)
        for h in (1, 0):
            part[h * ROWS : (h + 1) * ROWS] = product(h)
            for u in range(2):
                pass_on(0, h, u, False)

    start2(4)

    for j in (1, 2, 3):
        arrived(j)
        right(j)
        for h in (1, 0):
            part[h * ROWS : (h + 1) * ROWS] = product(h)
            if j == 1:
                for u in range(2):
                    pass_on(j, h, u, h == 0)
        if j > 1:
            for h in (1, 0):
                for u in range(2):
                    pass_on(j, h, u, True)

    @pl.when(core == 1)
    def _():
        arrived(4)
        right(4)
        part[ROWS : 2 * ROWS] = product(1)
        own_copy.start()
        result[...] = product(0)

    @pl.when(core == 0)
    def _():
        own_copy.wait_recv()

    stores = []
    for u in range(2):
        rows = slice(u * SUB, (u + 1) * SUB)
        v = result[rows]
        for c in range(2):
            at_ = (c, u)
            v = v + came_in(fq.at[at_], fs.at[at_], rfq.at[at_], rfs.at[at_])
        total[rows] = v
        stores.append(pltpu.make_async_copy(total.at[rows], out_hbm.at[rows], out_sem.at[u]))
        stores[u].start()

    lam_copy.wait_send()
    for g in range(5):
        for t in (1, 2, 3):
            phase1(g, t, b).wait_send()
        if g in (0, 4):
            split_by_core(
                g,
                lambda: [phase2(g, o, t).wait_send() for o, t in same] and None,
                lambda: [phase2(g, o, t).wait_send() for o, t in other] and None,
            )
        else:
            for o, t in same + other:
                phase2(g, o, t).wait_send()

    @pl.when(core == 0)
    def _():
        for h in range(2):
            for u in range(2):
                for copy in sends(0, h, u):
                    copy.wait_send()

    @pl.when(core == 1)
    def _():
        own_copy.wait_send()

    for j in (1, 2, 3):
        for h in range(2):
            for u in range(2):
                for copy in sends(j, h, u):
                    copy.wait_send()
    for store in stores:
        store.wait()


def per_device(lambda_amp, lambda_tiles, integrals, integral_tiles):
    dma = pltpu.SemaphoreType.DMA
    hbm = pl.BlockSpec(memory_space=pl.ANY)
    return pl.pallas_call(
        kernel,
        out_shape=jax.ShapeDtypeStruct((ROWS, W), F32),
        in_specs=[hbm] * 4,
        out_specs=hbm,
        scratch_shapes=[
            pltpu.VMEM((ROWS, W), F32),
            pltpu.VMEM((3, ROWS), I32),
            pltpu.VMEM((12, 8 * W), F32),
            pltpu.SMEM((24, 24), I32),
            pltpu.VMEM((ROWS, W), F32),
            pltpu.VMEM((5, 4, 3, 8, W), F32),
            pltpu.VMEM((5, 6, 8, W), F32),
            pltpu.VMEM((5, 2, 4, 6, 8, W), F32),
            pltpu.VMEM((2 * ROWS, 4 * W), BF16),
            pltpu.VMEM((2 * ROWS, 2 * W), BF16),
            pltpu.VMEM((4 * W, W), BF16),
            pltpu.VMEM((2 * ROWS, W), F32),
            pltpu.VMEM((ROWS, W), F32),
            pltpu.VMEM((ROWS, W), F32),
            pltpu.VMEM((4, 2, 2, SUB, W), I16),
            pltpu.VMEM((4, 2, 2, 1, W), F32),
            pltpu.VMEM((3, 2, 2, SUB, W), I16),
            pltpu.VMEM((3, 2, 2, 1, W), F32),
            pltpu.VMEM((2, 2, SUB, W), I16),
            pltpu.VMEM((2, 2, 1, W), F32),
            dma((4,)),
            dma((2,)),
            dma((5, 3)),
            dma((5, 4)),
            dma((5, 2, 4)),
            dma((5, 2, 4)),
            dma,
            dma,
            dma,
            dma,
            dma((4, 2, 2)),
            dma((4, 2, 2)),
            dma((3, 2, 2)),
            dma((3, 2, 2)),
            dma((2, 2)),
            dma((2, 2)),
        ],
        compiler_params=pltpu.CompilerParams(
            collective_id=0, has_side_effects=True, vmem_limit_bytes=60 << 20
        ),
        cost_estimate=pl.CostEstimate(flops=3_700_000_000, bytes_accessed=1_500_000, transcendentals=0),
    )(lambda_amp, lambda_tiles.T, integrals, integral_tiles)


def solution(mesh):
    placed = (P("own", "rep"), P("own", "rep"), P(("rep", "own"), None), P())
    return jax.shard_map(
        per_device, mesh=mesh, in_specs=placed, out_specs=P("own", "rep"), check_vma=False
    )
```

time: 47 us -> 40.6 us (0.86); the launches traced: 46.9 us -> 40 us
  Pallas kernels: 43.3 us -> 38.2 us
  local copies, waits for them, and re-layouts: 3.5 us -> 1.77 us
    pallas_call x1, Pallas kernels: 43.3 us -> 38.2 us  [per_device(): pl.pallas_call(kernel, out_shape=jax.ShapeDtypeStruct((ROWS, W), F32), in...]
    unnamed x8 -> x1, local copies, waits for them, and re-layouts: 3.5 us -> 1.77 us
where the time goes in v2:
time: 40.6 us; the launch traced here: 40 us
  Pallas kernels  38.2 us (94%)
  local copies, waits for them, and re-layouts  1.77 us (4%)
    pallas_call x1, Pallas kernels, per_device(): pl.pallas_call(kernel, out_shape=jax.ShapeDtypeStruct((ROWS, W), F32), in...  38.2 us
    unnamed x1, local copies, waits for them, and re-layouts  1.77 us

profile of v2, /device:TPU:1, one launch (start us, length us, event | category | flops | bytes accessed | tf_op | source)
XLA Modules:
  0.0 40.0 jit_solution(14278922321227128182)
XLA Ops:
  0.0 38.2 %shard_map.46 = f32[256,384]{1,0:T(8,128)} custom-call(f32[256,384]{1,0:T(8,128)} %lam_hbm.1, s32[3,256]{1,0:T(4,128)} %bitcast.1, f32[12,3072]{1,0:T(8,128)} %ints_hbm.1, s32[24,24]{1,0:T(8,128)} %flags_hbm.1), custom_call_target="tpu_custom_call" | custom-call | flops 3700000000 | bytes 1500000 | tf_op jit(solution)/shard_map/pallas_call | solution.py:336
  38.2 1.8 %copy.6 = f32[256,384]{1,0:T(8,128)} copy(f32[256,384]{1,0:T(8,128)} %shard_map.46) | data formatting | bytes 786432

commit v3 on v2

--- a/solution.py
+++ b/solution.py
@@ -265,13 +265,8 @@
         right(j)
         for h in (1, 0):
             part[h * ROWS : (h + 1) * ROWS] = product(h)
-            if j == 1:
-                for u in range(2):
-                    pass_on(j, h, u, h == 0)
-        if j > 1:
-            for h in (1, 0):
-                for u in range(2):
-                    pass_on(j, h, u, True)
+            for u in range(2):
+                pass_on(j, h, u, j > 1 or h == 0)
 
     @pl.when(core == 1)
     def _():
@@ -285,16 +280,13 @@
     def _():
         own_copy.wait_recv()
 
-    stores = []
     for u in range(2):
         rows = slice(u * SUB, (u + 1) * SUB)
         v = result[rows]
         for c in range(2):
             at_ = (c, u)
             v = v + came_in(fq.at[at_], fs.at[at_], rfq.at[at_], rfs.at[at_])
-        total[rows] = v
-        stores.append(pltpu.make_async_copy(total.at[rows], out_hbm.at[rows], out_sem.at[u]))
-        stores[u].start()
+        out_hbm[rows] = v
 
     lam_copy.wait_send()
     for g in range(5):
@@ -326,8 +318,6 @@
             for u in range(2):
                 for copy in sends(j, h, u):
                     copy.wait_send()
-    for store in stores:
-        store.wait()
 
 
 def per_device(lambda_amp, lambda_tiles, integrals, integral_tiles):
@@ -335,9 +325,9 @@
     hbm = pl.BlockSpec(memory_space=pl.ANY)
     return pl.pallas_call(
         kernel,
-        out_shape=jax.ShapeDtypeStruct((ROWS, W), F32),
+        out_shape=pltpu.VMEM((ROWS, W), F32),
         in_specs=[hbm] * 4,
-        out_specs=hbm,
+        out_specs=pl.BlockSpec(memory_space=pltpu.VMEM),
         scratch_shapes=[
             pltpu.VMEM((ROWS, W), F32),
             pltpu.VMEM((3, ROWS), I32),
@@ -377,10 +367,10 @@
             dma((2, 2)),
         ],
         compiler_params=pltpu.CompilerParams(
-            collective_id=0, has_side_effects=True, vmem_limit_bytes=60 << 20
+            collective_id=0, has_side_effects=True, vmem_limit_bytes=48 << 20
         ),
         cost_estimate=pl.CostEstimate(flops=3_700_000_000, bytes_accessed=1_500_000, transcendentals=0),
-    )(lambda_amp, lambda_tiles.T, integrals, integral_tiles)
+    )(*(pltpu.with_memory_space_constraint(v, pltpu.HBM) for v in (lambda_amp, lambda_tiles.T, integrals, integral_tiles)))
 
 
 def solution(mesh):

time: 40.6 us -> 39 us (0.961)
  local copies, waits for them, and re-layouts: 1.77 us -> 0.75 us
  Pallas kernels: 38.2 us -> 37.6 us
    unnamed x1, local copies, waits for them, and re-layouts: 1.77 us -> 0.75 us
    pallas_call x1, Pallas kernels: 38.2 us -> 37.6 us  [per_device(): pl.pallas_call(kernel, out_shape=pltpu.VMEM((ROWS, W), F32), in_specs=[hb...]
where the time goes in v3:
time: 39 us; the launch traced here: 38.4 us
  Pallas kernels  37.6 us (96%)
  local copies, waits for them, and re-layouts  0.75 us (2%)
    pallas_call x1, Pallas kernels, per_device(): pl.pallas_call(kernel, out_shape=pltpu.VMEM((ROWS, W), F32), in_specs=[hb...  37.6 us

profile of v3, /device:TPU:1, one launch (start us, length us, event | category | flops | bytes accessed | tf_op | source)
XLA Modules:
  0.0 38.4 jit_solution(13210275399515910405)
XLA Ops:
  0.0 37.6 %shard_map.46 = f32[256,384]{1,0:T(8,128)S(1)} custom-call(f32[256,384]{1,0:T(8,128)} %lam_hbm.1, s32[3,256]{1,0:T(4,128)} %bitcast.1, f32[12,3072]{1,0:T(8,128)} %ints_hbm.1, s32[24,24]{1,0:T(8,128)} %flags_hbm.1), custom_call_target="tpu_custom_call" | custom-call | flops 3700000000 | bytes 1500000 | tf_op jit(solution)/shard_map/pallas_call | solution.py:326
  37.6 0.7 %copy.6 = f32[256,384]{1,0:T(8,128)} copy(f32[256,384]{1,0:T(8,128)S(1)} %shard_map.46) | data formatting | bytes 786432

commit v4 on v3

--- a/solution.py
+++ b/solution.py
@@ -115,7 +115,7 @@
         return remote(rows, rows, s1.at[g, t - 1], r1.at[g, slot], at(0, 0, t, core))
 
     def start1(g):
-        for t in (1, 3, 2):
+        for t in (2, 1, 3):
             phase1(g, t, b).start()
 
     def phase2(g, o, t):
@@ -127,7 +127,7 @@
         device = at(0, t, 0, c) if o == 0 else at(0, 0, t, c)
         return remote(gath.at[g, c, slot], gath.at[g, c, slot], s2.at[g, o, t], r2.at[g, c, slot], device)
 
-    same, other = ((0, 1), (0, 3), (0, 2)), ((1, 1), (1, 3), (1, 2), (1, 0))
+    same, other = ((0, 2), (0, 1), (0, 3)), ((1, 2), (1, 1), (1, 3), (1, 0))
     low = lax.broadcasted_iota(I32, (8, W), 0) < 4
     mine_first = (lax.broadcasted_iota(I32, (8, W), 0) < 4) == (core == 0)
 
@@ -157,10 +157,11 @@
                 lambda: [phase2(g, o, t).start() for o, t in other] and None,
             )
         else:
-            for o, t in same + other:
+            for o, t in ((0, 2), (1, 2), (0, 1), (1, 1), (0, 3), (1, 3), (1, 0)):
                 phase2(g, o, t).start()
 
     def arrived(g):
+        return
         for o, t in same + other:
             phase2_came(g, o, t).wait_recv()
 
@@ -208,10 +209,13 @@
     prepare(lamx[...], 1)
 
     def right(g):
-        for i in range(8):
-            r1_, r2_, r3_ = split3(gath[g, i // 4, i % 4].reshape(48, W))
+        for o, t in ((0, 0), (1, 0), (0, 1), (0, 3), (1, 1), (1, 3), (0, 2), (1, 2)):
+            c, slot = (core, lax.rem(a + t, 4)) if o == 0 else (1 - core, lax.rem(b + t, 4))
+            if o or t:
+                phase2_came(g, o, t).wait_recv()
+            r1_, r2_, r3_ = split3(gath[g, c, slot].reshape(48, W))
             for k, s in enumerate((r1_, r2_, r3_, r1_)):
-                ra[k * W + i * 48 : k * W + (i + 1) * 48] = s
+                ra[pl.ds(pl.multiple_of(k * W + (c * 4 + slot) * 48, 16), 48)] = s
 
     def product(h):
         rows = slice(h * ROWS, (h + 1) * ROWS)
@@ -275,18 +279,6 @@
         part[ROWS : 2 * ROWS] = product(1)
         own_copy.start()
         result[...] = product(0)
-
-    @pl.when(core == 0)
-    def _():
-        own_copy.wait_recv()
-
-    for u in range(2):
-        rows = slice(u * SUB, (u + 1) * SUB)
-        v = result[rows]
-        for c in range(2):
-            at_ = (c, u)
-            v = v + came_in(fq.at[at_], fs.at[at_], rfq.at[at_], rfs.at[at_])
-        out_hbm[rows] = v
 
     lam_copy.wait_send()
     for g in range(5):
@@ -309,15 +301,32 @@
                 for copy in sends(0, h, u):
                     copy.wait_send()
 
-    @pl.when(core == 1)
-    def _():
-        own_copy.wait_send()
-
-    for j in (1, 2, 3):
+    for j in (1, 2):
         for h in range(2):
             for u in range(2):
                 for copy in sends(j, h, u):
                     copy.wait_send()
+
+    @pl.when(core == 0)
+    def _():
+        own_copy.wait_recv()
+
+    for u in range(2):
+        rows = slice(u * SUB, (u + 1) * SUB)
+        v = result[rows]
+        for c in range(2):
+            at_ = (c, u)
+            v = v + came_in(fq.at[at_], fs.at[at_], rfq.at[at_], rfs.at[at_])
+        out_hbm[rows] = v
+
+    @pl.when(core == 1)
+    def _():
+        own_copy.wait_send()
+
+    for h in range(2):
+        for u in range(2):
+            for copy in sends(3, h, u):
+                copy.wait_send()
 
 
 def per_device(lambda_amp, lambda_tiles, integrals, integral_tiles):

time: 39 us -> 38.6 us (0.990)
  no operation moved by 1% of the time
where the time goes in v4:
time: 38.6 us; the launch traced here: 38.1 us
  Pallas kernels  37.3 us (97%)
  local copies, waits for them, and re-layouts  0.75 us (2%)
    pallas_call x1, Pallas kernels, per_device(): pl.pallas_call(kernel, out_shape=pltpu.VMEM((ROWS, W), F32), in_specs=[hb...  37.3 us

profile of v4, /device:TPU:1, one launch (start us, length us, event | category | flops | bytes accessed | tf_op | source)
XLA Modules:
  0.0 38.1 jit_solution(5386892000847508185)
XLA Ops:
  0.0 37.3 %shard_map.46 = f32[256,384]{1,0:T(8,128)S(1)} custom-call(f32[256,384]{1,0:T(8,128)} %lam_hbm.1, s32[3,256]{1,0:T(4,128)} %bitcast.1, f32[12,3072]{1,0:T(8,128)} %ints_hbm.1, s32[24,24]{1,0:T(8,128)} %flags_hbm.1), custom_call_target="tpu_custom_call" | custom-call | flops 3700000000 | bytes 1500000 | tf_op jit(solution)/shard_map/pallas_call | solution.py:335
  37.3 0.7 %copy.6 = f32[256,384]{1,0:T(8,128)} copy(f32[256,384]{1,0:T(8,128)S(1)} %shard_map.46) | data formatting | bytes 786432

commit v5 on v4

--- a/solution.py
+++ b/solution.py
@@ -61,9 +61,9 @@
         )
 
     barrier = pltpu.get_barrier_semaphore()
-    peers = [at(0, t, 0, 1 - core) for t in range(4)] + [at(0, 0, t, 1 - core) for t in (1, 2, 3)]
-    peers += [at(0, t, 0, core) for t in (1, 2, 3)] + [at(0, 0, t, core) for t in (1, 2, 3)]
-    peers += [at(d, 0, 0, c) for d in (1, -1) for c in (core, 1 - core)]
+    peers = [at(0, t, 0, c) for t in (2, 1, 3) for c in (core, 1 - core)]
+    peers += [at(0, 0, t, c) for t in (2, 1, 3) for c in (core, 1 - core)]
+    peers += [at(d, 0, 0, c) for d in (1, -1) for c in (core, 1 - core)] + [at(0, 0, 0, 1 - core)]
     for peer in peers:
         pl.semaphore_signal(barrier, inc=1, device_id=peer, device_id_type=MESH)
 
@@ -107,8 +107,8 @@
                 came[g, b, 1 - odd, :, to] = v[0:8]
                 came[g, b, 2, 4:8, to] = v[8:12]
 
-    for g in range(5):
-        pack(g)
+    pack(0)
+    pack(1)
 
     def phase1(g, t, slot):
         rows = came.at[g, slot, pl.ds(1, 2)] if g in (0, 4) else came.at[g, slot]
@@ -160,16 +160,14 @@
             for o, t in ((0, 2), (1, 2), (0, 1), (1, 1), (0, 3), (1, 3), (1, 0)):
                 phase2(g, o, t).start()
 
-    def arrived(g):
-        return
-        for o, t in same + other:
-            phase2_came(g, o, t).wait_recv()
-
     lam_copy = remote(lam, lamx, sl, rl, at(0, 0, 0, 1 - core))
 
     pl.semaphore_wait(barrier, len(peers))
     start1(0)
     start1(1)
+    for g in (2, 3, 4):
+        pack(g)
+        start1(g)
 
     loads[2].wait()
     loads[3].wait()
@@ -178,9 +176,6 @@
         cols = slice(u * TILE, (u + 1) * TILE)
         lam[:, cols] = lam[:, cols] * kept[:, u : u + 1]
     lam_copy.start()
-    start1(2)
-    start1(3)
-    start1(4)
 
     n = lax.broadcasted_iota(I32, (1, W), 1)
     origin = (n >= 192).astype(I32)
@@ -203,7 +198,7 @@
             lb[rows, i * W : (i + 1) * W] = l2
 
     prepare(lam[...], 0)
-    for g in range(4):
+    for g in range(3):
         start2(g)
     lam_copy.wait_recv()
     prepare(lamx[...], 1)
@@ -255,17 +250,16 @@
 
     @pl.when(core == 0)
     def _():
-        arrived(0)
         right(0)
         for h in (1, 0):
             part[h * ROWS : (h + 1) * ROWS] = product(h)
             for u in range(2):
                 pass_on(0, h, u, False)
 
+    start2(3)
     start2(4)
 
     for j in (1, 2, 3):
-        arrived(j)
         right(j)
         for h in (1, 0):
             part[h * ROWS : (h + 1) * ROWS] = product(h)
@@ -274,7 +268,6 @@
 
     @pl.when(core == 1)
     def _():
-        arrived(4)
         right(4)
         part[ROWS : 2 * ROWS] = product(1)
         own_copy.start()

time: 38.6 us -> 38.6 us (level)
  no operation moved by 1% of the time
where the time goes in v5:
time: 38.6 us; the launch traced here: 38 us
  Pallas kernels  37.3 us (97%)
  local copies, waits for them, and re-layouts  0.75 us (2%)
    pallas_call x1, Pallas kernels, per_device(): pl.pallas_call(kernel, out_shape=pltpu.VMEM((ROWS, W), F32), in_specs=[hb...  37.3 us

profile of v5, /device:TPU:1, one launch (start us, length us, event | category | flops | bytes accessed | tf_op | source)
XLA Modules:
  0.0 38.0 jit_solution(16983630564494714981)
XLA Ops:
  0.0 37.3 %shard_map.46 = f32[256,384]{1,0:T(8,128)S(1)} custom-call(f32[256,384]{1,0:T(8,128)} %lam_hbm.1, s32[3,256]{1,0:T(4,128)} %bitcast.1, f32[12,3072]{1,0:T(8,128)} %ints_hbm.1, s32[24,24]{1,0:T(8,128)} %flags_hbm.1), custom_call_target="tpu_custom_call" | custom-call | flops 3700000000 | bytes 1500000 | tf_op jit(solution)/shard_map/pallas_call | solution.py:328
  37.3 0.7 %copy.6 = f32[256,384]{1,0:T(8,128)} copy(f32[256,384]{1,0:T(8,128)S(1)} %shard_map.46) | data formatting | bytes 786432

commit v6 on v4

--- a/solution.py
+++ b/solution.py
@@ -35,8 +35,8 @@
 def kernel(
     lam_hbm, keep_hbm, ints_hbm, flags_hbm, out_hbm,
     lam, keep, ints, flags, lamx, came, relay, gath, la, lb, ra, part, result, total,
-    sq, ss, rq, rs, fq, fs,
-    in_sem, out_sem, s1, r1, s2, r2, sl, rl, so, ro, szq, szs, rzq, rzs, rfq, rfs,
+    sq, ss, rq, rs,
+    in_sem, out_sem, s1, r1, s2, r2, sl, rl, so, ro, szq, szs, rzq, rzs,
 ):
     z = lax.axis_index("rep")
     own = lax.axis_index("own")
@@ -160,11 +160,6 @@
             for o, t in ((0, 2), (1, 2), (0, 1), (1, 1), (0, 3), (1, 3), (1, 0)):
                 phase2(g, o, t).start()
 
-    def arrived(g):
-        return
-        for o, t in same + other:
-            phase2_came(g, o, t).wait_recv()
-
     lam_copy = remote(lam, lamx, sl, rl, at(0, 0, 0, 1 - core))
 
     pl.semaphore_wait(barrier, len(peers))
@@ -223,58 +218,62 @@
         return most + jnp.dot(lb[rows], ra[0 : 2 * W], preferred_element_type=F32)
 
     def sends(j, h, u):
-        if j < 3:
-            target = at(step, 0, 0, core) if j else at(1 - 2 * h, 0, 0, h)
-            hh = h if j else 0
-            to = (rq.at[j, hh, u], rs.at[j, hh, u], rzq.at[j, hh, u], rzs.at[j, hh, u])
+        if isinstance(j, int) and j == 0:
+            target, hh = at(1 - 2 * h, 0, 0, h), 0
         else:
-            target = at(step, 0, 0, core if h == 0 else 1 - core)
-            to = (fq.at[core, u], fs.at[core, u], rfq.at[core, u], rfs.at[core, u])
+            last = j // 3
+            target = at(step, 0, 0, core + last * h * (1 - 2 * core))
+            hh = h + last * (core - h)
         return (
-            remote(sq.at[j, h, u], to[0], szq.at[j, h, u], to[2], target),
-            remote(ss.at[j, h, u], to[1], szs.at[j, h, u], to[3], target),
+            remote(sq.at[j, h, u], rq.at[j, hh, u], szq.at[j, h, u], rzq.at[j, hh, u], target),
+            remote(ss.at[j, h, u], rs.at[j, hh, u], szs.at[j, h, u], rzs.at[j, hh, u], target),
         )
 
-    def came_in(q_ref, s_ref, q_sem, s_sem):
-        for ref, sem in ((q_ref, q_sem), (s_ref, s_sem)):
-            remote(ref, ref, szq.at[3, 0, 0], sem, at(step, 0, 0, core)).wait_recv()
-        return decode(q_ref[...], s_ref[...])
-
-    def pass_on(j, h, u, add):
+    def came_in(j, h, u):
+        for ref, sem in ((rq, rzq), (rs, rzs)):
+            remote(ref.at[j, h, u], ref.at[j, h, u], szq.at[3, 0, 0], sem.at[j, h, u], at(step, 0, 0, core)).wait_recv()
+
+    def pass_on(j, h, u):
         v = part[(h * 2 + u) * SUB : (h * 2 + u + 1) * SUB]
-        if add:
-            at_ = (j - 1, h, u)
-            v = v + came_in(rq.at[at_], rs.at[at_], rzq.at[at_], rzs.at[at_])
+        if not isinstance(j, int):
+            if h == 1:
+                pl.when(j > 1)(lambda: came_in(j - 1, h, u))
+            else:
+                came_in(j - 1, h, u)
+            v = v + decode(rq[j - 1, h, u], rs[j - 1, h, u])
         code, scale = encode(v)
         sq[j, h, u] = code
         ss[j, h, u] = scale
         for copy in sends(j, h, u):
             copy.start()
 
+    rq[0, 1] = jnp.zeros((2, SUB, W), I16)
+    rs[0, 1] = jnp.zeros((2, 1, W), F32)
+
     own_copy = remote(part.at[pl.ds(ROWS, ROWS)], result, so, ro, at(0, 0, 0, 1 - core))
 
     @pl.when(core == 0)
     def _():
-        arrived(0)
         right(0)
         for h in (1, 0):
             part[h * ROWS : (h + 1) * ROWS] = product(h)
             for u in range(2):
-                pass_on(0, h, u, False)
+                pass_on(0, h, u)
 
     start2(4)
 
-    for j in (1, 2, 3):
-        arrived(j)
+    def ring_step(j, carry):
         right(j)
         for h in (1, 0):
             part[h * ROWS : (h + 1) * ROWS] = product(h)
             for u in range(2):
-                pass_on(j, h, u, j > 1 or h == 0)
+                pass_on(j, h, u)
+        return carry
+
+    lax.fori_loop(1, 4, ring_step, 0)
 
     @pl.when(core == 1)
     def _():
-        arrived(4)
         right(4)
         part[ROWS : 2 * ROWS] = product(1)
         own_copy.start()
@@ -315,8 +314,8 @@
         rows = slice(u * SUB, (u + 1) * SUB)
         v = result[rows]
         for c in range(2):
-            at_ = (c, u)
-            v = v + came_in(fq.at[at_], fs.at[at_], rfq.at[at_], rfs.at[at_])
+            came_in(3, c, u)
+            v = v + decode(rq[3, c, u], rs[3, c, u])
         out_hbm[rows] = v
 
     @pl.when(core == 1)
@@ -354,10 +353,8 @@
             pltpu.VMEM((ROWS, W), F32),
             pltpu.VMEM((4, 2, 2, SUB, W), I16),
             pltpu.VMEM((4, 2, 2, 1, W), F32),
-            pltpu.VMEM((3, 2, 2, SUB, W), I16),
-            pltpu.VMEM((3, 2, 2, 1, W), F32),
-            pltpu.VMEM((2, 2, SUB, W), I16),
-            pltpu.VMEM((2, 2, 1, W), F32),
+            pltpu.VMEM((4, 2, 2, SUB, W), I16),
+            pltpu.VMEM((4, 2, 2, 1, W), F32),
             dma((4,)),
             dma((2,)),
             dma((5, 3)),
@@ -370,10 +367,8 @@
             dma,
             dma((4, 2, 2)),
             dma((4, 2, 2)),
-            dma((3, 2, 2)),
-            dma((3, 2, 2)),
-            dma((2, 2)),
-            dma((2, 2)),
+            dma((4, 2, 2)),
+            dma((4, 2, 2)),
         ],
         compiler_params=pltpu.CompilerParams(
             collective_id=0, has_side_effects=True, vmem_limit_bytes=48 << 20

time: 38.6 us -> 38.7 us (level)
  no operation moved by 1% of the time
where the time goes in v6:
time: 38.7 us; the launch traced here: 38.1 us
  Pallas kernels  37.4 us (97%)
  local copies, waits for them, and re-layouts  0.75 us (2%)
    pallas_call x1, Pallas kernels, per_device(): pl.pallas_call(kernel, out_shape=pltpu.VMEM((ROWS, W), F32), in_specs=[hb...  37.4 us

profile of v6, /device:TPU:1, one launch (start us, length us, event | category | flops | bytes accessed | tf_op | source)
XLA Modules:
  0.0 38.1 jit_solution(2928480633734361006)
XLA Ops:
  0.0 37.4 %shard_map.46 = f32[256,384]{1,0:T(8,128)S(1)} custom-call(f32[256,384]{1,0:T(8,128)} %lam_hbm.1, s32[3,256]{1,0:T(4,128)} %bitcast.1, f32[12,3072]{1,0:T(8,128)} %ints_hbm.1, s32[24,24]{1,0:T(8,128)} %flags_hbm.1), custom_call_target="tpu_custom_call" | custom-call | flops 3700000000 | bytes 1500000 | tf_op jit(solution)/shard_map/pallas_call | solution.py:334
  37.4 0.7 %copy.6 = f32[256,384]{1,0:T(8,128)} copy(f32[256,384]{1,0:T(8,128)S(1)} %shard_map.46) | data formatting | bytes 786432
